TPU v7x, 512 devices: a whole 4x4x16 slice. The times are simulated.
512 devices in a mesh: band: 32 (over y, x, z_hi), tracer: 16 (over z_lo, core).
Axes of the slice: x: 4, y: 4, z: 16 (z_hi: 2, z_lo: 8; z = z_hi * 8 + z_lo), core: 2. Of those that a mesh axis runs over, the one named last changes fastest.
Arguments:
- tracer: float32 [16, 16, 256, 720], P(None, 'tracer', 'band'), may hold values from 0.1 to 10
- air_mass: bfloat16 [16, 16, 256, 720], P('tracer', None, 'band'), may hold values from 1 to 2
- fluxes: bfloat16 [16, 3, 16, 256, 720], P('tracer', None, None, 'band'), may hold values from -0.119628906 to 0.119628906
- diffusivity: bfloat16 [16, 16, 256, 720], P('tracer', None, 'band'), may hold values from 0.29882812 to 3
- input_slot: int32 [32], replicated, may hold values from 0 to 15, as said below
Outputs:
- new_tracer: float32 [16, 16, 256, 720], P(None, 'tracer', 'band')
Inputs may be any that keep to these rules, and one draw needn't show every extreme that they name: `input_slot`: band b reads slot (b + s) mod 16, with one s for all bands.
All inputs are finite; a program needn't handle non-finite values.
Results may differ from a plain program's by a relative error of at most 0.0003.
Values may be sent and summed in bfloat16 or wider, within the bound.
A program may use at most 64 MiB of HBM per device.

v0:
```python
import jax
import jax.numpy as jnp
from jax import lax
from jax.sharding import PartitionSpec as P


def from_root(block, axis, holder):
    block = jnp.where(lax.axis_index(axis) == holder, block, jnp.zeros_like(block))
    return lax.psum(block, axis)


def extended(x, sides, width):
    for axis, dim in sides:
        count, length = (lax.axis_size(axis), x.shape[dim])
        up = [(i, (i + 1) % count) for i in range(count - 1)]
        down = [(j, i) for i, j in up]
        last = lax.slice_in_dim(x, length - width, length, axis=dim)
        leading = lax.slice_in_dim(x, 0, width, axis=dim)
        before = lax.ppermute(last, axis, up)
        after = lax.ppermute(leading, axis, down)
        x = jnp.concatenate([before, x, after], axis=dim)
    return x


def from_behind(block, axis, distance):
    devices = range(lax.axis_size(axis))
    route = [(i - distance, i) for i in devices if i - distance in devices]
    return lax.ppermute(block, axis, route)


def limited_slope(left, centre, right):
    down = centre - left
    rise = right - centre
    middle = 0.5 * (right - left)
    bound = jnp.minimum(jnp.minimum(jnp.abs(middle), 2.0 * jnp.abs(down)), 2.0 * jnp.abs(rise))
    return jnp.where(down * rise > 0.0, jnp.sign(down) * bound, 0.0)


def part_of(array, axis, lower, upper):
    return lax.slice_in_dim(array, lower, upper, axis=axis)


def advect(conc, mass, flux, axis):
    count = conc.shape[axis] - 4
    slope = limited_slope(
        part_of(conc, axis, 0, count + 2),
        part_of(conc, axis, 1, count + 3),
        part_of(conc, axis, 2, count + 4),
    )
    face = part_of(flux, axis, 1, count + 2)
    left_c = part_of(conc, axis, 1, count + 2)
    right_c = part_of(conc, axis, 2, count + 3)
    left_m = part_of(mass, axis, 1, count + 2)
    right_m = part_of(mass, axis, 2, count + 3)
    left_s = part_of(slope, axis, 0, count + 1)
    right_s = part_of(slope, axis, 1, count + 2)
    forward = face * (left_c + 0.5 * (1.0 - face / left_m) * left_s)
    backward = face * (right_c - 0.5 * (1.0 + face / right_m) * right_s)
    moved = jnp.where(face > 0.0, forward, backward)
    inner_m = part_of(mass, axis, 2, count + 2)
    inner_c = part_of(conc, axis, 2, count + 2)
    new_mass = inner_m + part_of(face, axis, 0, count) - part_of(face, axis, 1, count + 1)
    new_amount = (
        inner_m * inner_c + part_of(moved, axis, 0, count) - part_of(moved, axis, 1, count + 1)
    )
    return (new_amount / new_mass, new_mass)


def wrap_x(array):
    return jnp.concatenate([array[..., -2:], array, array[..., :2]], axis=3)


def pad_axis(array, axis, value):
    widths = [(0, 0)] * array.ndim
    widths[axis] = (2, 2)
    return jnp.pad(array, widths, constant_values=value)


def diffuse(conc, mass, coupling):
    below = jnp.concatenate([jnp.zeros_like(coupling[:1]), coupling[:-1]], axis=0)
    diag = mass + below + coupling
    right_side = mass * conc

    def forward(carry, level):
        ratio_prev, value_prev = carry
        low, centre, upper_c, known = level
        pivot = centre - low * ratio_prev
        ratio = upper_c / pivot
        value = (known + low * value_prev) / pivot
        return ((ratio, value), (ratio, value))

    start = (jnp.zeros(mass.shape[1:], jnp.float32), jnp.zeros(conc.shape[1:], jnp.float32))
    _, (ratios, values) = lax.scan(forward, start, (below, diag, coupling, right_side), unroll=8)

    def backward(above, level):
        ratio, value = level
        result = value + ratio * above
        return (result, result)

    _, solved = lax.scan(
        backward, jnp.zeros(conc.shape[1:], jnp.float32), (ratios, values), reverse=True, unroll=8
    )
    return solved


def per_device(tracer, air_mass, fluxes, diffusivity, input_slot):
    levels = tracer.shape[0]
    species = tracer.shape[1]
    rows_here = tracer.shape[2]
    bands = input_slot.shape[0]
    band_id = lax.axis_index("band")
    root = jnp.sum(jnp.where(jnp.arange(bands) == band_id, input_slot, 0))
    first_row = band_id * rows_here
    total_rows = bands * rows_here
    row_ids = first_row + jnp.arange(rows_here)
    mass_b, flux_b, coupling_b = (
        from_root(air_mass[0], "tracer", root),
        from_root(fluxes[0], "tracer", root),
        from_root(diffusivity[0], "tracer", root),
    )
    east_b = flux_b[0]
    north_b = flux_b[1]
    upper_b = flux_b[2]
    row_keep = (row_ids < total_rows - 1)[None, :, None]
    north_kept = jnp.where(row_keep, north_b, jnp.zeros_like(north_b))
    wide_ids = first_row - 2 + jnp.arange(rows_here + 4)
    inside = ((wide_ids >= 0) & (wide_ids < total_rows))[None, None, :, None]
    mass0 = mass_b.astype(jnp.float32)[:, None]
    east = east_b.astype(jnp.float32)[:, None]
    conc1, mass1 = advect(wrap_x(tracer), wrap_x(mass0), wrap_x(east), 3)
    stacked = jnp.concatenate([conc1, mass1], axis=1)
    wide = extended(stacked, (("band", 2),), 2)
    below_row = from_behind(north_kept[:, rows_here - 1 :], "band", 1)
    north_full = jnp.concatenate(
        [
            jnp.zeros_like(below_row),
            below_row,
            north_kept,
            jnp.zeros_like(below_row),
            jnp.zeros_like(below_row),
        ],
        axis=1,
    )
    conc_wide = wide[:, :species]
    mass_wide = wide[:, species : species + 1]
    north_wide = north_full.astype(jnp.float32)[:, None]
    mass_wide = jnp.where(inside, mass_wide, 1.0)
    conc2, mass2 = advect(conc_wide, mass_wide, north_wide, 2)
    level_keep = (jnp.arange(levels) < levels - 1)[:, None, None, None]
    upper = jnp.where(level_keep, upper_b.astype(jnp.float32)[:, None], 0.0)
    coupling = jnp.where(level_keep, coupling_b.astype(jnp.float32)[:, None], 0.0)
    conc3, mass3 = advect(
        pad_axis(conc2, 0, 0.0), pad_axis(mass2, 0, 1.0), pad_axis(upper, 0, 0.0), 0
    )
    return diffuse(conc3, mass3, coupling)


def solution(mesh):
    placed = (
        P(None, "tracer", "band", None),
        P("tracer", None, "band", None),
        P("tracer", None, None, "band", None),
        P("tracer", None, "band", None),
        P(),
    )
    return jax.shard_map(
        per_device,
        mesh=mesh,
        in_specs=placed,
        out_specs=P(None, "tracer", "band", None),
        check_vma=False,
    )
```

profile of v0, /device:TPU:7, one launch (start us, length us, event | category | flops | bytes accessed | tf_op | source)
XLA Modules:
  0.0 271.8 jit_solution(5897603894556639427)
XLA Ops:
  6.5 1.3 fusion.96
  8.5 2.0 fusion.61
  10.6 0.7 fusion.94
  11.3 0.7 fusion.95
  12.1 0.1 copy.43
  12.3 0.1 pad.23.clone
  12.4 0.1 fusion.123
  12.5 0.4 multiply_select_fusion.2
  12.9 199.9 %all-reduce.7.cloned.1.call-done = (bf16[16,8,720]{2,0,1:T(8,128)(2,1)}, bf16[3,16,8,720]{3,1,2,0:T(8,128)(2,1)}, bf16[16,1,8,720]{3,0,2,1:T(8,128)(2,1)}) async-done(((bf16[16,8,720]{2,0,1:T(8,128)(2,1)}, bf16[3,16,8,720]{3,1,2,0:T(8,128)(2,1)}, bf16[16,1,8,720]{3,0,2,1:T(8,128)(2,1)}), (bf16[16,8,720]{2,0,1:T(8,128)(2,1)}, bf16[3,16,8,720]{3,1,2,0:T(8,128)(2,1)}, ...) | async-done | bytes 921616 | tf_op jit(solution)/shard_map/psum | solution.py:9
  212.8 0.9 fusion.124
  213.7 1.0 broadcast_in_dim.211
  214.7 1.0 fusion.93
  215.6 0.1 fusion.92
  215.7 0.1 fusion.125
  215.8 0.1 slice.580
  215.9 0.6 fusion.74
  216.5 0.4 copy-done.1
  216.8 0.4 fusion.84
  217.2 7.8 %collective-permute-start.2 = (bf16[16,1,720]{2,0,1:T(8,128)(2,1)S(1)}, bf16[16,1,720]{2,0,1:T(8,128)(2,1)S(1)}, u32[]{:S(2)}, u32[]{:S(2)}) collective-permute-start(bf16[16,1,720]{2,0,1:T(8,128)(2,1)S(1)} %slice.598), channel_id=1, source_target_pairs={{0,16},{16,32},{32,48},{48,64},{64,80},{80,96},{96,112},{112,128},... | collective-permute-start | bytes 69128 | tf_op jit(solution)/shard_map/ppermute | solution.py:28
  225.1 0.1 convert_select_fusion
  225.2 0.1 convert_select_fusion.1
  225.4 7.1 %collective-permute-start = (f32[16,2,2,720]{3,0,2,1:T(8,128)S(1)}, f32[16,2,2,720]{3,0,2,1:T(8,128)S(1)}, u32[]{:S(2)}, u32[]{:S(2)}) collective-permute-start(f32[16,2,2,720]{3,0,2,1:T(8,128)S(1)} %get-tuple-element.331), channel_id=1, source_target_pairs={{0,16},{16,32},{32,48},{48,64},{64,80},{80,96},{96,112},{112,128},... | collective-permute-start | bytes 552968 | tf_op jit(solution)/shard_map/ppermute | solution.py:19
  232.5 7.8 %collective-permute-start.1 = (f32[16,2,2,720]{3,0,2,1:T(8,128)S(1)}, f32[16,2,2,720]{3,0,2,1:T(8,128)S(1)}, u32[]{:S(2)}, u32[]{:S(2)}) collective-permute-start(f32[16,2,2,720]{3,0,2,1:T(8,128)S(1)} %get-tuple-element.332), channel_id=1, source_target_pairs={{16,0},{32,16},{48,32},{64,48},{80,64},{96,80},{112,96},{128,112},... | collective-permute-start | bytes 552968 | tf_op jit(solution)/shard_map/ppermute | solution.py:20
  240.3 4.6 %collective-permute-done.2 = bf16[16,1,720]{2,0,1:T(8,128)(2,1)S(1)} collective-permute-done((bf16[16,1,720]{2,0,1:T(8,128)(2,1)S(1)}, bf16[16,1,720]{2,0,1:T(8,128)(2,1)S(1)}, u32[]{:S(2)}, u32[]{:S(2)}) %collective-permute-start.2) | collective-permute-done | bytes 23072 | tf_op jit(solution)/shard_map/ppermute | solution.py:28
  244.9 0.1 maximum_convert_fusion
  245.0 10.1 %collective-permute-done = f32[16,2,2,720]{3,0,2,1:T(8,128)S(1)} collective-permute-done((f32[16,2,2,720]{3,0,2,1:T(8,128)S(1)}, f32[16,2,2,720]{3,0,2,1:T(8,128)S(1)}, u32[]{:S(2)}, u32[]{:S(2)}) %collective-permute-start) | collective-permute-done | bytes 184352 | tf_op jit(solution)/shard_map/ppermute | solution.py:19
  255.2 4.0 %collective-permute-done.1 = f32[16,2,2,720]{3,0,2,1:T(8,128)S(1)} collective-permute-done((f32[16,2,2,720]{3,0,2,1:T(8,128)S(1)}, f32[16,2,2,720]{3,0,2,1:T(8,128)S(1)}, u32[]{:S(2)}, u32[]{:S(2)}) %collective-permute-start.1) | collective-permute-done | bytes 184352 | tf_op jit(solution)/shard_map/ppermute | solution.py:20
  259.1 0.1 pad_maximum_fusion
  259.2 0.1 slice_select_fusion
  259.3 0.1 pad_maximum_fusion.1
  259.4 0.4 multiply_select_fusion.1
  259.8 0.2 fusion.64
  260.0 0.1 fusion.81
  260.2 0.5 multiply_select_fusion
  260.7 0.5 fusion.54
  261.1 0.3 fusion.78
  261.5 2.3 while.34
  261.5 0.2 constant_dynamic-slice_fusion.36
  261.7 0.2 constant_dynamic-slice_fusion.37
  261.9 0.2 constant_dynamic-slice_fusion.38
  262.1 0.2 constant_dynamic-slice_fusion.39
  262.7 0.2 constant_dynamic-slice_fusion.36
  262.8 0.2 constant_dynamic-slice_fusion.37
  263.0 0.2 constant_dynamic-slice_fusion.38
  263.2 0.2 constant_dynamic-slice_fusion.39
  263.8 0.4 while.35
  263.9 0.1 bitcast_dynamic-update-slice_fusion.22
  264.2 0.7 copy-done.4
  (79 shorter events, 0.9 us)
Async XLA Ops:
  6.5 4.0 %copy-start.5 = (bf16[1,16,8,720]{3,2,1,0:T(8,128)(2,1)S(1)}, bf16[1,16,8,720]{3,2,1,0:T(8,128)(2,1)}, u32[]{:S(2)}) copy-start(bf16[1,16,8,720]{3,2,1,0:T(8,128)(2,1)} %param.10) | copy-start | bytes 552964
  6.5 4.8 %copy-start.6 = (bf16[1,16,8,720]{3,2,1,0:T(8,128)(2,1)S(1)}, bf16[1,16,8,720]{3,2,1,0:T(8,128)(2,1)}, u32[]{:S(2)}) copy-start(bf16[1,16,8,720]{3,2,1,0:T(8,128)(2,1)} %param.12) | copy-start | bytes 552964
  6.5 206.2 %all-reduce.7.cloned.1.call-start = ((), (), s32[]{:S(2)}) async-start(), calls=%async_computation | async-start | bytes 1966080 | tf_op jit(solution)/shard_map/psum | solution.py:9
  10.6 1.5 copy-start
  212.8 2.8 %copy-start.2 = (bf16[3,16,8,720]{3,1,2,0:T(8,128)(2,1)S(1)}, bf16[3,16,8,720]{3,1,2,0:T(8,128)(2,1)}, u32[]{:S(2)}) copy-start(bf16[3,16,8,720]{3,1,2,0:T(8,128)(2,1)} %get-tuple-element.255) | copy-start | bytes 1658884
  215.9 0.9 copy-start.1
  216.8 8.4 %copy-start.3 = (bf16[16,8,720]{2,0,1:T(8,128)(2,1)S(1)}, bf16[16,8,720]{2,0,1:T(8,128)(2,1)}, u32[]{:S(2)}) copy-start(bf16[16,8,720]{2,0,1:T(8,128)(2,1)} %get-tuple-element.254) | copy-start | bytes 552964
  217.2 27.7 %collective-permute-start.2 = (bf16[16,1,720]{2,0,1:T(8,128)(2,1)S(1)}, bf16[16,1,720]{2,0,1:T(8,128)(2,1)S(1)}, u32[]{:S(2)}, u32[]{:S(2)}) collective-permute-start(bf16[16,1,720]{2,0,1:T(8,128)(2,1)S(1)} %slice.598), channel_id=1, source_target_pairs={{0,16},{16,32},{32,48},{48,64},{64,80},{80,96},{96,112},{112,128},... | collective-permute-start | bytes 69128 | tf_op jit(solution)/shard_map/ppermute | solution.py:28
  225.4 29.8 %collective-permute-start = (f32[16,2,2,720]{3,0,2,1:T(8,128)S(1)}, f32[16,2,2,720]{3,0,2,1:T(8,128)S(1)}, u32[]{:S(2)}, u32[]{:S(2)}) collective-permute-start(f32[16,2,2,720]{3,0,2,1:T(8,128)S(1)} %get-tuple-element.331), channel_id=1, source_target_pairs={{0,16},{16,32},{32,48},{48,64},{64,80},{80,96},{96,112},{112,128},... | collective-permute-start | bytes 552968 | tf_op jit(solution)/shard_map/ppermute | solution.py:19
  232.5 26.7 %collective-permute-start.1 = (f32[16,2,2,720]{3,0,2,1:T(8,128)S(1)}, f32[16,2,2,720]{3,0,2,1:T(8,128)S(1)}, u32[]{:S(2)}, u32[]{:S(2)}) collective-permute-start(f32[16,2,2,720]{3,0,2,1:T(8,128)S(1)} %get-tuple-element.332), channel_id=1, source_target_pairs={{16,0},{32,16},{48,32},{64,48},{80,64},{96,80},{112,96},{128,112},... | collective-permute-start | bytes 552968 | tf_op jit(solution)/shard_map/ppermute | solution.py:20
  264.2 0.7 copy-start.4
Sparse Core Ops, SparseCore 0:
  12.2 200.5 all-reduce.6
where the time goes:
time: 273 us; the launch traced here: 272 us
  waiting for transfers between devices  219 us (80%)
  starting transfers between devices  22.7 us (8%)
  between operations  14.3 us (5%)
  other arithmetic  11.5 us (4%)
  local copies, waits for them, and re-layouts  4.16 us (2%)
    psum x1, waiting for transfers between devices, from_root(): return lax.psum(block, axis)  200 us
    ppermute x1, waiting for transfers between devices, extended(): before = lax.ppermute(last, axis, up)  10.1 us
    ppermute x1, starting transfers between devices, from_behind(): return lax.ppermute(block, axis, route)  7.85 us
    ppermute x1, starting transfers between devices, extended(): after = lax.ppermute(leading, axis, down)  7.84 us
    ppermute x1, starting transfers between devices, extended(): before = lax.ppermute(last, axis, up)  7.06 us
  transfers between devices with their start and end apart: 4, of which 4 were waited for; matrix products, arithmetic and copies ran while one was open for 0% of the time, Pallas kernels for 0%

commit v1 on v0

v1 whole, which is shorter than its diff:
```python
import functools

import jax
import jax.numpy as jnp
from jax import lax
from jax.experimental import pallas as pl
from jax.experimental.pallas import tpu as pltpu
from jax.sharding import PartitionSpec as P

MESH = pl.DeviceIdType.MESH
LEV = 16
ROWS = 8
LON = 720
WIDE = 768
LANE = 128
BANDS = 32
SLOTS = 16
CHIPS = 8
CELLS = LEV * ROWS
CHUNK = 4
PER_FIELD = LEV // CHUNK
NCHUNK = 5 * PER_FIELD
BELOW = 5
ABOVE = 4


def row_plane(stage, row):
    parts = [stage[j, pl.ds(row, LEV, stride=ROWS), :] for j in range(WIDE // LANE)]
    parts[-1] = parts[-1][:, :LON % LANE]
    return jnp.concatenate(parts, axis=1).astype(jnp.bfloat16)


def fill_stage(stage, field):
    for j in range(WIDE // LANE):
        width = min(LANE, LON - j * LANE)
        stage[j, :, :width] = field[:, j * LANE:j * LANE + width]


def comm_kernel(
    shift, x_ref, mass_ref, flux_ref, coup_ref, met, edge, halo,
    hsend, esend, stage, local_sem, main_recv, main_send, halo_sem, edge_recv, edge_send,
):
    b = lax.axis_index("band")
    t = lax.axis_index("tracer")
    z = t // 2
    c = t % 2
    root = (b + shift) % SLOTS
    k = root // 2
    root_core = root % 2
    is_root = t == root
    at_root = z == k
    mate = t + 1 - 2 * c
    has_below = b > 0
    has_above = b < BANDS - 1
    side = jnp.where(z >= k, 1, -1)
    pos = jnp.where(z >= k, z - k, k - z)
    length = jnp.where(z >= k, CHIPS - 1 - k, k)
    hub = jnp.logical_and(pos > 0, pos % 2 == 0)
    child_far = jnp.logical_and(hub, pos + 2 <= length)
    child_back = hub
    child_last = jnp.logical_and(hub, pos + 1 == length)
    odd_parent = jnp.where(pos < length, pos + 1, pos - 1)
    parent_pos = jnp.where(pos % 2 == 0, pos - 2, odd_parent)
    parent_z = k + side * parent_pos
    up_step = jnp.minimum(CHIPS - 1 - k, 2)
    down_step = jnp.minimum(k, 2)
    root_up = jnp.logical_and(is_root, up_step > 0)
    root_down = jnp.logical_and(is_root, down_step > 0)
    one = lambda flag: jnp.where(flag, 1, 0)

    edge_hub = jnp.logical_or(z == 2, z == 5)
    hub_z = jnp.where(z < 4, 2, 5)
    far_z = jnp.where(z == 2, 0, 7)

    barrier = pltpu.get_barrier_semaphore()

    def greet(band, tracer, flag=None):
        def go():
            pl.semaphore_signal(barrier, inc=1, device_id={"band": band, "tracer": tracer}, device_id_type=MESH)

        if flag is None:
            go()
        else:
            pl.when(flag)(go)

    greet(b, mate)
    main_parent = jnp.where(parent_z == k, root, parent_z * 2 + c)
    greet(b, main_parent, jnp.logical_not(at_root))
    greet(b - 1, t, has_below)
    greet(b + 1, t, has_above)
    greet(b, hub_z * 2 + c, jnp.logical_not(edge_hub))
    greet(b - 1, (root + SLOTS - 1) % SLOTS, edge_hub & (c == 0) & has_below)
    greet(b + 1, (root + 1) % SLOTS, edge_hub & (c == 1) & has_above)
    expect = (
        1
        + one(has_below) + one(has_above)
        + one(child_far) + one(child_back) + one(child_last)
        + 2 * one(root_up) + 2 * one(root_down)
        + 3 * one(edge_hub)
        + 2 * one(is_root & has_below) + 2 * one(is_root & has_above)
    )

    loads = (
        pltpu.make_async_copy(mass_ref.at[0], met.at[0], local_sem.at[0]),
        pltpu.make_async_copy(flux_ref.at[0], met.at[pl.ds(1, 3)], local_sem.at[1]),
        pltpu.make_async_copy(coup_ref.at[0], met.at[4], local_sem.at[2]),
    )

    @pl.when(is_root)
    def _():
        for load in loads:
            load.start()

    pl.semaphore_wait(barrier, expect)

    def piece(i):
        return met.at[i // PER_FIELD, pl.ds(i % PER_FIELD * CHUNK, CHUNK)]

    def main_copy(i, which, tracer):
        return pltpu.make_async_remote_copy(
            src_ref=piece(i), dst_ref=piece(i),
            send_sem=main_send.at[which, i], recv_sem=main_recv.at[i],
            device_id={"band": b, "tracer": tracer}, device_id_type=MESH,
        )

    def start_if(flag, copy):
        pl.when(flag)(copy.start)

    @pl.when(is_root)
    def _():
        for load in loads:
            load.wait()

        def send(i, _):
            core = i % 2
            start_if(root_up, main_copy(i, 0, (z + up_step) * 2 + core))
            start_if(root_down, main_copy(i, 1, (z - down_step) * 2 + core))
            main_copy(i, 3, mate).start()
            return 0

        lax.fori_loop(0, NCHUNK, send, 0)

    fill_stage(stage, x_ref[...].reshape(CELLS, LON))
    for plane, row in enumerate((ROWS - 2, ROWS - 1, 0, 1)):
        hsend[plane] = row_plane(stage, row)

    def halo_copy(lower, band):
        part = pl.ds(0 if lower else 2, 2)
        return pltpu.make_async_remote_copy(
            src_ref=hsend.at[part], dst_ref=halo.at[part],
            send_sem=halo_sem.at[0 if lower else 1], recv_sem=halo_sem.at[2 if lower else 3],
            device_id={"band": band, "tracer": t}, device_id_type=MESH,
        )

    to_above = halo_copy(True, b + 1)
    to_below = halo_copy(False, b - 1)
    start_if(has_above, to_above)
    start_if(has_below, to_below)

    below_part = pl.ds(0, BELOW)
    above_part = pl.ds(BELOW, ABOVE)

    def edge_copy(which, lower, band, tracer, own):
        part = below_part if lower else above_part
        source = (esend if own else edge).at[part]
        return pltpu.make_async_remote_copy(
            src_ref=source, dst_ref=edge.at[part],
            send_sem=edge_send.at[which], recv_sem=edge_recv.at[0 if lower else 1],
            device_id={"band": band, "tracer": tracer}, device_id_type=MESH,
        )

    edge_out = (
        (is_root & has_above, edge_copy(0, True, b + 1, 4, True)),
        (is_root & has_above, edge_copy(1, True, b + 1, 10, True)),
        (is_root & has_below, edge_copy(2, False, b - 1, 5, True)),
        (is_root & has_below, edge_copy(3, False, b - 1, 11, True)),
    )

    @pl.when(is_root)
    def _():
        plan = (
            (0, ((ROWS - 2, 0), (ROWS - 1, 1), (0, 5), (1, 6))),
            (1, ((ROWS - 2, 2), (ROWS - 1, 3), (0, 7), (1, 8))),
            (2, ((ROWS - 1, 4),)),
        )
        for field, places in plan:
            fill_stage(stage, met[field].astype(jnp.float32).reshape(CELLS, LON))
            for row, place in places:
                esend[place] = row_plane(stage, row)
        for flag, copy in edge_out:
            start_if(flag, copy)

    relay = jnp.logical_not(at_root)

    def handed(i):
        return (
            (child_far, main_copy(i, 0, (z + 2 * side) * 2 + c)),
            (child_back, main_copy(i, 1, (z - side) * 2 + c)),
            (child_last, main_copy(i, 2, (z + side) * 2 + c)),
            (relay, main_copy(i, 3, mate)),
        )

    @pl.when(relay)
    def _():
        def step(j, _):
            i = 2 * j + c
            main_copy(i, 0, mate).wait_recv()
            for flag, copy in handed(i):
                start_if(flag, copy)
            return 0

        lax.fori_loop(0, NCHUNK // 2, step, 0)

    def edge_relay(lower):
        return (
            (edge_hub, edge_copy(4, lower, b, (z - 1) * 2 + c, False)),
            (edge_hub, edge_copy(5, lower, b, (z + 1) * 2 + c, False)),
            (edge_hub, edge_copy(6, lower, b, far_z * 2 + c, False)),
            (None, edge_copy(7, lower, b, mate, False)),
        )

    for lower, present in ((True, has_below), (False, has_above)):
        @pl.when(present & (c == (0 if lower else 1)))
        def _(lower=lower):
            edge_copy(0, lower, b, mate, False).wait_recv()
            for flag, copy in edge_relay(lower):
                if flag is None:
                    copy.start()
                else:
                    start_if(flag, copy)

    for lower, present in ((True, has_below), (False, has_above)):
        @pl.when(present & (c == (1 if lower else 0)))
        def _(lower=lower):
            edge_copy(0, lower, b, mate, False).wait_recv()

        @pl.when(present & (c == (0 if lower else 1)))
        def _(lower=lower):
            for flag, copy in edge_relay(lower):
                if flag is None:
                    copy.wait_send()
                else:
                    pl.when(flag)(copy.wait_send)

    pl.when(has_below)(to_above.wait_recv)
    pl.when(has_above)(to_below.wait_recv)
    pl.when(has_above)(to_above.wait_send)
    pl.when(has_below)(to_below.wait_send)
    for flag, copy in edge_out:
        pl.when(flag)(copy.wait_send)

    @pl.when(is_root)
    def _():
        def done(i, _):
            pl.when(root_up)(main_copy(i, 0, mate).wait_send)
            pl.when(root_down)(main_copy(i, 1, mate).wait_send)
            main_copy(i, 3, mate).wait_send()
            return 0

        lax.fori_loop(0, NCHUNK, done, 0)

    @pl.when(relay)
    def _():
        def done(j, _):
            main_copy(2 * j + 1 - c, 0, mate).wait_recv()
            for flag, copy in handed(2 * j + c):
                pl.when(flag)(copy.wait_send)
            return 0

        lax.fori_loop(0, NCHUNK // 2, done, 0)

    @pl.when(at_root & jnp.logical_not(is_root))
    def _():
        def done(i, _):
            main_copy(i, 0, mate).wait_recv()
            return 0

        lax.fori_loop(0, NCHUNK, done, 0)


def comm(shift, tracer, mass, flux, coup):
    vmem = pl.BlockSpec(memory_space=pltpu.VMEM)
    hbm = pl.BlockSpec(memory_space=pl.ANY)
    return pl.pallas_call(
        functools.partial(comm_kernel, shift),
        out_shape=(
            jax.ShapeDtypeStruct((5, LEV, ROWS, LON), jnp.bfloat16),
            jax.ShapeDtypeStruct((BELOW + ABOVE, LEV, LON), jnp.bfloat16),
            jax.ShapeDtypeStruct((4, LEV, LON), jnp.bfloat16),
        ),
        in_specs=[vmem, hbm, hbm, hbm],
        out_specs=(vmem, vmem, vmem),
        scratch_shapes=[
            pltpu.VMEM((4, LEV, LON), jnp.bfloat16),
            pltpu.VMEM((BELOW + ABOVE, LEV, LON), jnp.bfloat16),
            pltpu.VMEM((WIDE // LANE, CELLS, LANE), jnp.float32),
            pltpu.SemaphoreType.DMA((3,)),
            pltpu.SemaphoreType.DMA((NCHUNK,)),
            pltpu.SemaphoreType.DMA((4, NCHUNK)),
            pltpu.SemaphoreType.DMA((4,)),
            pltpu.SemaphoreType.DMA((2,)),
            pltpu.SemaphoreType.DMA((8,)),
        ],
        compiler_params=pltpu.CompilerParams(
            collective_id=shift, has_side_effects=True, vmem_limit_bytes=24 << 20
        ),
        name="exchange",
    )(tracer, mass, flux, coup)


def extended(x):
    spare = (WIDE - LON) // 2
    return jnp.concatenate([x, x[:, :spare], x[:, LON - spare:]], axis=1)


def doubled_slope(down, rise):
    middle = down + rise
    down, rise = 4.0 * down, 4.0 * rise
    positive = jnp.maximum(jnp.minimum(jnp.minimum(middle, down), rise), 0.0)
    negative = jnp.minimum(jnp.maximum(jnp.maximum(middle, down), rise), 0.0)
    return positive + negative


def advect_x(conc, mass, east):
    left = lambda v: pltpu.roll(v, 1, 1)
    right = lambda v: pltpu.roll(v, WIDE - 1, 1)
    rise = right(conc) - conc
    slope = doubled_slope(left(rise), rise)
    inverse = 1.0 / mass
    west = left(east)
    ahead = conc + 0.25 * (1.0 - east * inverse) * slope
    behind = conc - 0.25 * (1.0 + west * inverse) * slope
    moved = east * jnp.where(east > 0.0, ahead, right(behind))
    new_mass = mass + west - east
    new_amount = mass * conc + left(moved) - moved
    return new_amount / new_mass, new_mass


def compute_kernel(x_ref, met, edge, halo, out, conc2, mass2, ratio, value, side_c, side_m, side_f):
    b = lax.axis_index("band")
    f32 = jnp.float32
    lowest, highest = b == 0, b == BANDS - 1

    def plane(i):
        return extended(edge[i].astype(f32))

    for at, mass_at, east_at, out_of in ((0, 0, 2, lowest), (1, 1, 3, lowest), (2, 5, 7, highest), (3, 6, 8, highest)):
        conc, mass = advect_x(extended(halo[at].astype(f32)), plane(mass_at), plane(east_at))
        side_c[at] = jnp.where(out_of, 0.0, conc)
        if at in (1, 2):
            side_m[at - 1] = jnp.where(out_of, 1.0, mass)
    side_f[...] = jnp.where(lowest, 0.0, plane(4))

    row = lax.broadcasted_iota(jnp.int32, (ROWS, WIDE), 0)
    first, last = row == 0, row == ROWS - 1
    sign = jnp.where(first, 1.0, -1.0)
    closed = jnp.logical_and(last, highest)

    def horizontal(lev, _):
        def field(i):
            return extended(met[i, lev].astype(f32))

        def spread(ref, *at):
            return jnp.broadcast_to(ref[(*at, pl.ds(lev, 1), slice(None))].reshape(1, WIDE), (ROWS, WIDE))

        conc, mass = advect_x(extended(x_ref[lev]), field(0), field(1))
        north = jnp.where(closed, 0.0, field(2))
        c_before, c_after = spread(side_c, 1), spread(side_c, 2)
        f_before = spread(side_f)
        lower = lambda v: pltpu.roll(v, 1, 0)
        higher = lambda v: pltpu.roll(v, ROWS - 1, 0)
        down = conc - jnp.where(first, c_before, lower(conc))
        rise = jnp.where(last, c_after, higher(conc)) - conc
        slope = doubled_slope(down, rise)
        inverse = 1.0 / mass
        south = jnp.where(first, f_before, lower(north))
        ahead = conc + 0.25 * (1.0 - north * inverse) * slope
        behind = conc - 0.25 * (1.0 + south * inverse) * slope
        c_out = jnp.where(first, c_before, c_after)
        low_out = jnp.where(last, conc, spread(side_c, 0))
        high_out = jnp.where(first, conc, spread(side_c, 3))
        f_out = jnp.where(first, f_before, north)
        m_out = jnp.where(first, spread(side_m, 0), spread(side_m, 1))
        s_out = doubled_slope(c_out - low_out, high_out - c_out)
        from_out = c_out + 0.25 * (sign - f_out / m_out) * s_out
        moved = north * jnp.where(north > 0.0, ahead, jnp.where(last, from_out, higher(behind)))
        entering = f_before * jnp.where(f_before > 0.0, from_out, behind)
        new_mass = mass + south - north
        new_amount = mass * conc + jnp.where(first, entering, lower(moved)) - moved
        conc2[lev] = new_amount / new_mass
        mass2[lev] = new_mass
        return 0

    lax.fori_loop(0, LEV, horizontal, 0)
    zero = jnp.zeros((ROWS, WIDE), f32)
    for beyond in range(2):
        conc2[LEV + beyond] = zero
    mass2[LEV] = zero + 1.0

    def vertical(lev, carry):
        slope, c_below, flux_below, moved_below, k_below, ratio_prev, value_prev = carry
        inside = lev < LEV - 1
        flux = jnp.where(inside, extended(met[3, lev].astype(f32)), 0.0)
        k_above = jnp.where(inside, extended(met[4, lev].astype(f32)), 0.0)
        conc, above = conc2[lev], conc2[lev + 1]
        mass, mass_above = mass2[lev], mass2[lev + 1]
        slope_above = doubled_slope(above - conc, conc2[lev + 2] - above)
        up = flux > 0.0
        upwind_m = jnp.where(up, mass, mass_above)
        upwind_c = jnp.where(up, conc, above)
        upwind_s = jnp.where(up, slope, -slope_above)
        moved = flux * (upwind_c + 0.25 * (1.0 - jnp.abs(flux) / upwind_m) * upwind_s)
        new_mass = mass + flux_below - flux
        amount = mass * conc + moved_below - moved
        pivot = 1.0 / (new_mass + k_below + k_above - k_below * ratio_prev)
        ratio_here = k_above * pivot
        value_here = (amount + k_below * value_prev) * pivot
        ratio[lev] = ratio_here
        value[lev] = value_here
        return slope_above, conc, flux, moved, k_above, ratio_here, value_here

    first_slope = doubled_slope(conc2[0], conc2[1] - conc2[0])
    lax.fori_loop(0, LEV, vertical, (first_slope, zero, zero, zero, zero, zero, zero))

    def back(i, above):
        lev = LEV - 1 - i
        result = value[lev] + ratio[lev] * above
        out[lev] = result[:, :LON]
        return result

    lax.fori_loop(0, LEV, back, zero)


def compute(tracer, met, edge, halo):
    vmem = pl.BlockSpec(memory_space=pltpu.VMEM)
    f32 = jnp.float32
    return pl.pallas_call(
        compute_kernel,
        out_shape=jax.ShapeDtypeStruct((LEV, ROWS, LON), f32),
        in_specs=[vmem] * 4,
        out_specs=vmem,
        scratch_shapes=[
            pltpu.VMEM((LEV + 2, ROWS, WIDE), f32),
            pltpu.VMEM((LEV + 1, ROWS, WIDE), f32),
            pltpu.VMEM((LEV, ROWS, WIDE), f32),
            pltpu.VMEM((LEV, ROWS, WIDE), f32),
            pltpu.VMEM((4, LEV, WIDE), f32),
            pltpu.VMEM((2, LEV, WIDE), f32),
            pltpu.VMEM((LEV, WIDE), f32),
        ],
        compiler_params=pltpu.CompilerParams(vmem_limit_bytes=24 << 20),
        name="transport",
    )(tracer, met, edge, halo)


def per_device(tracer, air_mass, fluxes, diffusivity, input_slot):
    held = tracer.reshape(LEV, ROWS, LON)
    branches = [functools.partial(comm, shift) for shift in range(SLOTS)]
    met, edge, halo = lax.switch(input_slot[0], branches, held, air_mass, fluxes, diffusivity)
    return compute(held, met, edge, halo).reshape(tracer.shape)


def solution(mesh):
    placed = (
        P(None, "tracer", "band", None),
        P("tracer", None, "band", None),
        P("tracer", None, None, "band", None),
        P("tracer", None, "band", None),
        P(),
    )
    return jax.shard_map(
        per_device,
        mesh=mesh,
        in_specs=placed,
        out_specs=P(None, "tracer", "band", None),
        check_vma=False,
    )
```

time: 273 us -> 65.4 us (0.24)
  the two profiles are of different devices: /device:TPU:7 before, /device:TPU:19 now
where the time goes in v1:
time: 65.4 us; the launch traced here: 65.2 us
  Pallas kernels  64.5 us (99%)
    pallas_call x1, Pallas kernels, comm(): pl.pallas_call(functools.partial(comm_kernel, shift), out_shape=(jax.Shap...  53.7 us
    pallas_call x1, Pallas kernels, compute(): pl.pallas_call(compute_kernel, out_shape=jax.ShapeDtypeStruct((LEV, ROWS,...  10.8 us

profile of v1, /device:TPU:19, one launch (start us, length us, event | category | flops | bytes accessed | tf_op | source)
XLA Modules:
  0.0 65.2 jit_solution(9870726246728513886)
XLA Ops:
  0.0 0.0 copy-start
  0.0 0.7 %copy-done = s32[32]{0:T(128)S(1)} copy-done((s32[32]{0:T(128)S(1)}, s32[32]{0:T(128)}, u32[]{:S(2)}) %copy-start) | copy-done | bytes 152
  0.7 53.8 %conditional.1 = ((bf16[5,16,8,720]{3,2,1,0:T(8,128)(2,1)S(1)}, bf16[9,16,720]{2,1,0:T(8,128)(2,1)S(1)}, bf16[4,16,720]{2,1,0:T(8,128)(2,1)S(1)})) conditional(s32[]{:T(128)} %bitcast.1, (f32[16,8,720]{2,1,0:T(8,128)}, bf16[1,16,8,720]{3,2,1,0:T(8,128)(2,1)}, bf16[1,3,16,8,720]{4,3,2,1,0:T(8,128)(2,1)}, ...), branch_computations={%region_0.0_spmd, %region_1.0_spmd, %region_2.0_spmd, %region_3.0_... | conditional | bytes 8 | solution.py:459
  0.7 53.7 %exchange.28 = (bf16[5,16,8,720]{3,2,1,0:T(8,128)(2,1)S(1)}, bf16[9,16,720]{2,1,0:T(8,128)(2,1)S(1)}, bf16[4,16,720]{2,1,0:T(8,128)(2,1)S(1)}) custom-call(f32[16,8,720]{2,1,0:T(8,128)} %get-tuple-element.181.x_ref, bf16[1,16,8,720]{3,2,1,0:T(8,128)(2,1)} %get-tuple-element.182.mass_ref, bf16[1,3,16,8,720]{4,3,2,1,0:T(8,128)(2,1)} %get-tuple-element.183.flux_ref, ...), custom_call_target="tpu_custom_call" | custom-call | tf_op jit(solution)/shard_map/cond/branch_12_fun/exchange/pallas_call | solution.py:284
  54.5 10.8 %transport.1 = f32[16,8,720]{2,1,0:T(8,128)} custom-call(f32[16,8,720]{2,1,0:T(8,128)} %bitcast.22, bf16[5,16,8,720]{3,2,1,0:T(8,128)(2,1)S(1)} %get-tuple-element.200.met, bf16[9,16,720]{2,1,0:T(8,128)(2,1)S(1)} %get-tuple-element.201.edge, bf16[4,16,720]{2,1,0:T(8,128)(2,1)S(1)} %get-tuple-element.202.halo), custom_call_target="tpu_custom_call" | custom-call | tf_op jit(solution)/shard_map/transport/pallas_call | solution.py:437
Async XLA Ops:
  0.0 0.7 %copy-start = (s32[32]{0:T(128)S(1)}, s32[32]{0:T(128)}, u32[]{:S(2)}) copy-start(s32[32]{0:T(128)} %param.25) | copy-start | bytes 388

commit v2 on v0

v2 whole, which is shorter than its diff:
```python
import functools

import jax
import jax.numpy as jnp
from jax import lax
from jax.experimental import pallas as pl
from jax.experimental.pallas import tpu as pltpu
from jax.sharding import PartitionSpec as P

MESH = pl.DeviceIdType.MESH
LEV = 16
ROWS = 8
LON = 720
WIDE = 768
LANE = 128
BANDS = 32
SLOTS = 16
CHIPS = 8
CELLS = LEV * ROWS
CHUNK = 4
PER_FIELD = LEV // CHUNK
NCHUNK = 5 * PER_FIELD
BELOW = 5
ABOVE = 4


def extended(x):
    spare = (WIDE - LON) // 2
    return jnp.concatenate([x, x[:, :spare], x[:, LON - spare:]], axis=1)


def padded(x):
    return jnp.concatenate([x, jnp.zeros((x.shape[0], WIDE - LON), x.dtype)], axis=1)


def inverse_of(x):
    return pl.reciprocal(x, approx=True)


def doubled_slope(down, rise):
    middle = down + rise
    down, rise = 4.0 * down, 4.0 * rise
    positive = jnp.maximum(jnp.minimum(jnp.minimum(middle, down), rise), 0.0)
    negative = jnp.minimum(jnp.maximum(jnp.maximum(middle, down), rise), 0.0)
    return positive + negative


def advect_x(conc, mass, east):
    left = lambda v: pltpu.roll(v, 1, 1)
    right = lambda v: pltpu.roll(v, WIDE - 1, 1)
    rise = right(conc) - conc
    slope = 0.25 * doubled_slope(left(rise), rise)
    inverse = inverse_of(mass)
    west = left(east)
    ahead = conc + (1.0 - east * inverse) * slope
    behind = conc - (1.0 + west * inverse) * slope
    moved = east * jnp.where(east > 0.0, ahead, right(behind))
    new_mass = mass + west - east
    new_amount = mass * conc + left(moved) - moved
    inverse = inverse_of(new_mass)
    return new_amount * inverse, new_mass, inverse


def side_planes(edge, halo, side_c, side_i, side_f, lowest, highest):
    f32 = jnp.float32

    def plane(i):
        return extended(edge[i].astype(f32))

    for at, mass_at, east_at, out_of in ((0, 0, 2, lowest), (1, 1, 3, lowest), (2, 5, 7, highest), (3, 6, 8, highest)):
        conc, _, inverse = advect_x(extended(halo[at].astype(f32)), plane(mass_at), plane(east_at))
        side_c[at] = jnp.where(out_of, 0.0, conc)
        if at in (1, 2):
            side_i[at - 1] = jnp.where(out_of, 1.0, inverse)
    side_f[...] = jnp.where(lowest, 0.0, plane(4))


def longitude(lev, x_ref, met, conc1, mass1, inverse1):
    f32 = jnp.float32
    conc, mass, inverse = advect_x(
        extended(x_ref[lev]), extended(met[0, lev].astype(f32)), extended(met[1, lev].astype(f32))
    )
    conc1[lev] = conc
    mass1[lev] = mass
    inverse1[lev] = inverse


def latitude(lev, met, conc1, mass1, inverse1, side_c, side_i, side_f, highest):
    row = lax.broadcasted_iota(jnp.int32, (ROWS, WIDE), 0)
    first, last = row == 0, row == ROWS - 1

    def spread(ref, *at):
        return jnp.broadcast_to(ref[(*at, pl.ds(lev, 1), slice(None))].reshape(1, WIDE), (ROWS, WIDE))

    conc, mass, inverse = conc1[lev], mass1[lev], inverse1[lev]
    north = jnp.where(last & highest, 0.0, padded(met[2, lev].astype(jnp.float32)))
    c_before, c_after = spread(side_c, 1), spread(side_c, 2)
    f_before = spread(side_f)
    lower = lambda v: pltpu.roll(v, 1, 0)
    higher = lambda v: pltpu.roll(v, ROWS - 1, 0)
    down = conc - jnp.where(first, c_before, lower(conc))
    rise = jnp.where(last, c_after, higher(conc)) - conc
    slope = 0.25 * doubled_slope(down, rise)
    south = jnp.where(first, f_before, lower(north))
    ahead = conc + (1.0 - north * inverse) * slope
    behind = conc - (1.0 + south * inverse) * slope
    c_out = jnp.where(first, c_before, c_after)
    low_out = jnp.where(last, conc, spread(side_c, 0))
    high_out = jnp.where(first, conc, spread(side_c, 3))
    f_out = jnp.where(first, f_before, north)
    i_out = jnp.where(first, spread(side_i, 0), spread(side_i, 1))
    s_out = 0.25 * doubled_slope(c_out - low_out, high_out - c_out)
    from_out = c_out + (jnp.where(first, 1.0, -1.0) - f_out * i_out) * s_out
    moved = north * jnp.where(north > 0.0, ahead, jnp.where(last, from_out, higher(behind)))
    entering = f_before * jnp.where(f_before > 0.0, from_out, behind)
    new_mass = mass + south - north
    new_amount = mass * conc + jnp.where(first, entering, lower(moved)) - moved
    inverse = inverse_of(new_mass)
    return new_amount * inverse, new_mass, inverse


def vertical(lev, carry, met, conc2, mass2, inverse2, ratio, value):
    slope, flux_below, moved_below, k_below, ratio_prev, value_prev, conc, above, mass, inverse = carry
    f32 = jnp.float32
    inside = lev < LEV - 1
    flux = jnp.where(inside, padded(met[3, lev].astype(f32)), 0.0)
    k_above = jnp.where(inside, padded(met[4, lev].astype(f32)), 0.0)
    beyond = conc2[lev + 2]
    mass_above, inverse_above = mass2[lev + 1], inverse2[lev + 1]
    slope_above = 0.25 * doubled_slope(above - conc, beyond - above)
    up = flux > 0.0
    moved = flux * jnp.where(
        up, conc + (1.0 - flux * inverse) * slope, above - (1.0 + flux * inverse_above) * slope_above
    )
    amount = mass * conc + moved_below - moved
    pivot = inverse_of(mass + flux_below - flux + k_below * (1.0 - ratio_prev) + k_above)
    ratio_here = k_above * pivot
    value_here = (amount + k_below * value_prev) * pivot
    ratio[lev] = ratio_here
    value[lev] = value_here
    return slope_above, flux, moved, k_above, ratio_here, value_here, above, beyond, mass_above, inverse_above


def in_pairs(body, carry=None):
    def both(i, carry):
        carry = body(2 * i, carry)
        return body(2 * i + 1, carry)

    return lax.fori_loop(0, LEV // 2, both, carry)


def vertical_and_solve(met, out, conc2, mass2, inverse2, ratio, value):
    zero = jnp.zeros((ROWS, WIDE), jnp.float32)
    for beyond in range(2):
        conc2[LEV + beyond] = zero
    mass2[LEV] = zero
    inverse2[LEV] = zero
    first_slope = 0.25 * doubled_slope(conc2[0], conc2[1] - conc2[0])
    start = (first_slope, zero, zero, zero, zero, zero, conc2[0], conc2[1], mass2[0], inverse2[0])
    in_pairs(lambda lev, carry: vertical(lev, carry, met, conc2, mass2, inverse2, ratio, value), start)

    def back(i, above):
        lev = LEV - 1 - i
        result = value[lev] + ratio[lev] * above
        out[lev] = result[:, :LON]
        return result

    in_pairs(back, zero)


def row_plane(stage, row):
    parts = [stage[j, pl.ds(row, LEV, stride=ROWS), :] for j in range(WIDE // LANE)]
    parts[-1] = parts[-1][:, :LON % LANE]
    return jnp.concatenate(parts, axis=1).astype(jnp.bfloat16)


def fill_stage(stage, field):
    field = field.reshape(CELLS, LON)
    for j in range(WIDE // LANE):
        width = min(LANE, LON - j * LANE)
        stage[j, :, :width] = field[:, j * LANE:j * LANE + width]


def step_kernel(
    shift, x_hbm, mass_ref, flux_ref, coup_ref, out,
    x_ref, met, edge, halo, hsend, proxy, esend, stage,
    conc1, mass1, inverse1, conc2, mass2, inverse2, ratio, value, side_c, side_i, side_f,
    local_sem, main_recv, main_send, halo_recv, halo_send, proxy_sem, edge_recv, edge_send,
):
    b = lax.axis_index("band")
    t = lax.axis_index("tracer")
    z = t // 2
    c = t % 2
    root = (b + shift) % SLOTS
    k = root // 2
    line_core = root % 2
    relay = c == line_core
    speaker = c != line_core
    at_root = z == k
    is_root = relay & at_root
    passes = relay & jnp.logical_not(at_root)
    mate = t + 1 - 2 * c
    has_below = b > 0
    has_above = b < BANDS - 1

    side = jnp.where(z >= k, 1, -1)
    pos = jnp.where(z >= k, z - k, k - z)
    length = jnp.where(z >= k, CHIPS - 1 - k, k)
    hub = passes & (pos % 2 == 0)
    child_far = hub & (pos + 2 <= length)
    child_back = hub
    child_last = hub & (pos + 1 == length)
    odd_parent = jnp.where(pos < length, pos + 1, pos - 1)
    parent_pos = jnp.where(pos % 2 == 0, pos - 2, odd_parent)
    up_step = jnp.minimum(CHIPS - 1 - k, 2)
    down_step = jnp.minimum(k, 2)
    root_up = is_root & (up_step > 0)
    root_down = is_root & (down_step > 0)

    edge_hub = speaker & ((z == 2) | (z == 5))
    edge_leaf = speaker & (z != 2) & (z != 5)
    hub_z = jnp.where(z < 4, 2, 5)
    far_z = jnp.where(z == 2, 0, 7)
    tells = speaker & at_root

    def one(flag):
        return jnp.where(flag, 1, 0)

    barrier = pltpu.get_barrier_semaphore()

    def greet(band, tracer, flag=None):
        def go():
            pl.semaphore_signal(barrier, inc=1, device_id={"band": band, "tracer": tracer}, device_id_type=MESH)

        if flag is None:
            go()
        else:
            pl.when(flag)(go)

    def speaker_at_root(band):
        holder = (band + shift + SLOTS) % SLOTS
        return holder + 1 - 2 * (holder % 2)

    neighbour = jnp.where(relay, t, mate)
    greet(b, mate)
    greet(b, (k + side * parent_pos) * 2 + c, passes)
    greet(b - 1, neighbour, has_below)
    greet(b + 1, neighbour, has_above)
    greet(b, hub_z * 2 + c, edge_leaf)
    greet(b - 1, speaker_at_root(b - 1), edge_hub & has_below)
    greet(b + 1, speaker_at_root(b + 1), edge_hub & has_above)

    x_load = pltpu.make_async_copy(x_hbm, x_ref, local_sem.at[3])
    x_load.start()

    loads = (
        pltpu.make_async_copy(mass_ref.at[0], met.at[0], local_sem.at[0]),
        pltpu.make_async_copy(flux_ref.at[0], met.at[pl.ds(1, 3)], local_sem.at[1]),
        pltpu.make_async_copy(coup_ref.at[0], met.at[4], local_sem.at[2]),
    )

    @pl.when(is_root)
    def _():
        for load in loads:
            load.start()

    x_load.wait()
    fill_stage(stage, x_ref[...])
    for plane, row in enumerate((ROWS - 2, ROWS - 1, 0, 1)):
        hsend[plane] = row_plane(stage, row)

    neighbours = one(has_below) + one(has_above)
    pl.semaphore_wait(
        barrier,
        1
        + one(child_far) + one(child_back) + one(child_last)
        + one(root_up) + one(root_down)
        + 2 * one(speaker) * neighbours
        + 3 * one(edge_hub)
        + 2 * one(tells) * neighbours,
    )

    def remote(src, dst, send_sem, recv_sem, band, tracer):
        return pltpu.make_async_remote_copy(
            src_ref=src, dst_ref=dst, send_sem=send_sem, recv_sem=recv_sem,
            device_id={"band": band, "tracer": tracer}, device_id_type=MESH,
        )

    def main_copy(i, which, tracer):
        piece = met.at[i // PER_FIELD, pl.ds(i % PER_FIELD * CHUNK, CHUNK)]
        return remote(piece, piece, main_send.at[which, i], main_recv.at[i], b, tracer)

    def start_if(flag, copy):
        pl.when(flag)(copy.start)

    proxy_copy = remote(hsend, proxy, proxy_sem.at[0], proxy_sem.at[1], b, mate)

    @pl.when(is_root)
    def _():
        def send(i, _):
            start_if(root_up, main_copy(i, 0, (z + up_step) * 2 + c))
            start_if(root_down, main_copy(i, 1, (z - down_step) * 2 + c))
            main_copy(i, 3, mate).start()
            return 0

        for load, lower, upper in zip(loads, (0, 1, 4), (1, 4, 5), strict=True):
            load.wait()
            lax.fori_loop(lower * PER_FIELD, upper * PER_FIELD, send, 0)

    @pl.when(relay)
    def _():
        proxy_copy.start()

    def handed(i):
        return (
            (child_far, main_copy(i, 0, (z + 2 * side) * 2 + c)),
            (child_back, main_copy(i, 1, (z - side) * 2 + c)),
            (child_last, main_copy(i, 2, (z + side) * 2 + c)),
            (None, main_copy(i, 3, mate)),
        )

    def pass_on(i, _):
        main_copy(i, 0, mate).wait_recv()
        for flag, copy in handed(i):
            if flag is None:
                copy.start()
            else:
                start_if(flag, copy)
        return 0

    def levels(j, _):
        for lev in (2 * j, 2 * j + 1):
            longitude(lev, x_ref, met, conc1, mass1, inverse1)
        return 0

    @pl.when(passes)
    def _():
        lax.fori_loop(0, 2 * PER_FIELD, pass_on, 0)

        def both(j, _):
            pass_on(2 * PER_FIELD + j, 0)
            return levels(j, 0)

        lax.fori_loop(0, LEV // 2, both, 0)
        lax.fori_loop(2 * PER_FIELD + LEV // 2, NCHUNK, pass_on, 0)

    @pl.when(is_root)
    def _():
        lax.fori_loop(0, LEV // 2, levels, 0)

    def halo_copy(lower, own, band, tracer):
        part = pl.ds(0 if lower else 2, 2)
        return remote(
            (hsend if own else proxy).at[part], halo.at[part],
            halo_send.at[0 if own else 1, 0 if lower else 1], halo_recv.at[0 if lower else 1], band, tracer,
        )

    halos = tuple(
        (flag, halo_copy(lower, own, band, t if own else mate))
        for own in (True, False)
        for lower, band, flag in ((True, b + 1, has_above), (False, b - 1, has_below))
    )

    def edge_copy(which, lower, band, tracer, own):
        part = pl.ds(0, BELOW) if lower else pl.ds(BELOW, ABOVE)
        return remote(
            (esend if own else edge).at[part], edge.at[part],
            edge_send.at[which], edge_recv.at[0 if lower else 1], band, tracer,
        )

    edge_out = tuple(
        (tells & flag, edge_copy(which + (0 if lower else 1), lower, band, chip * 2 + line_core, True))
        for which, chip in ((0, 2), (2, 5))
        for lower, band, flag in ((True, b + 1, has_above), (False, b - 1, has_below))
    )

    def edge_relay(lower):
        first = 4 if lower else 8
        return (
            (edge_hub, edge_copy(first, lower, b, (z - 1) * 2 + c, False)),
            (edge_hub, edge_copy(first + 1, lower, b, (z + 1) * 2 + c, False)),
            (edge_hub, edge_copy(first + 2, lower, b, far_z * 2 + c, False)),
            (None, edge_copy(first + 3, lower, b, mate, False)),
        )

    sides = ((True, has_below), (False, has_above))

    @pl.when(speaker)
    def _():
        for flag, copy in halos[:2]:
            start_if(flag, copy)
        proxy_copy.wait_recv()
        for flag, copy in halos[2:]:
            start_if(flag, copy)

        @pl.when(at_root)
        def _():
            plan = (
                (0, ((ROWS - 2, 0), (ROWS - 1, 1), (0, 5), (1, 6))),
                (1, ((ROWS - 2, 2), (ROWS - 1, 3), (0, 7), (1, 8))),
                (2, ((ROWS - 1, 4),)),
            )
            for field, places in plan:
                for i in range(PER_FIELD):
                    main_copy(field * PER_FIELD + i, 0, mate).wait_recv()
                fill_stage(stage, met[field].astype(jnp.float32))
                for row, place in places:
                    esend[place] = row_plane(stage, row)
            for flag, copy in edge_out:
                start_if(flag, copy)

        for lower, present in sides:
            @pl.when(present)
            def _(lower=lower):
                edge_copy(0, lower, b, mate, False).wait_recv()
                for flag, copy in edge_relay(lower):
                    if flag is None:
                        copy.start()
                    else:
                        start_if(flag, copy)

        def arrived(i, _):
            main_copy(i, 0, mate).wait_recv()
            return 0

        first = jnp.where(at_root, 3 * PER_FIELD, 0)
        lax.fori_loop(first, jnp.maximum(first, 2 * PER_FIELD), arrived, 0)
        lax.fori_loop(0, LEV // 2, levels, 0)
        lax.fori_loop(jnp.maximum(first, 2 * PER_FIELD), NCHUNK, arrived, 0)

    @pl.when(relay)
    def _():
        for lower, present in sides:
            pl.when(present)(edge_copy(0, lower, b, mate, False).wait_recv)

    for lower, present in sides:
        pl.when(present)(halo_copy(lower, True, b, mate).wait_recv)

    lowest, highest = b == 0, b == BANDS - 1
    side_planes(edge, halo, side_c, side_i, side_f, lowest, highest)

    def across(i, _):
        for lev in (2 * i, 2 * i + 1):
            conc2[lev], mass2[lev], inverse2[lev] = latitude(
                lev, met, conc1, mass1, inverse1, side_c, side_i, side_f, highest
            )
        return 0

    lax.fori_loop(0, LEV // 2, across, 0)
    vertical_and_solve(met, out, conc2, mass2, inverse2, ratio, value)

    @pl.when(relay)
    def _():
        proxy_copy.wait_send()

    @pl.when(speaker)
    def _():
        for flag, copy in halos + edge_out:
            pl.when(flag)(copy.wait_send)
        for lower, present in sides:
            @pl.when(present)
            def _(lower=lower):
                for flag, copy in edge_relay(lower):
                    if flag is None:
                        copy.wait_send()
                    else:
                        pl.when(flag)(copy.wait_send)

    @pl.when(is_root)
    def _():
        def done(i, _):
            pl.when(root_up)(main_copy(i, 0, mate).wait_send)
            pl.when(root_down)(main_copy(i, 1, mate).wait_send)
            main_copy(i, 3, mate).wait_send()
            return 0

        lax.fori_loop(0, NCHUNK, done, 0)

    @pl.when(passes)
    def _():
        def done(i, _):
            for flag, copy in handed(i):
                if flag is None:
                    copy.wait_send()
                else:
                    pl.when(flag)(copy.wait_send)
            return 0

        lax.fori_loop(0, NCHUNK, done, 0)


def step(shift, tracer, mass, flux, coup):
    vmem = pl.BlockSpec(memory_space=pltpu.VMEM)
    hbm = pl.BlockSpec(memory_space=pl.ANY)
    bf16, f32 = jnp.bfloat16, jnp.float32
    return pl.pallas_call(
        functools.partial(step_kernel, shift),
        out_shape=jax.ShapeDtypeStruct((LEV, ROWS, LON), f32),
        in_specs=[hbm, hbm, hbm, hbm],
        out_specs=vmem,
        scratch_shapes=[
            pltpu.VMEM((LEV, ROWS, LON), f32),
            pltpu.VMEM((5, LEV, ROWS, LON), bf16),
            pltpu.VMEM((BELOW + ABOVE, LEV, LON), bf16),
            pltpu.VMEM((4, LEV, LON), bf16),
            pltpu.VMEM((4, LEV, LON), bf16),
            pltpu.VMEM((4, LEV, LON), bf16),
            pltpu.VMEM((BELOW + ABOVE, LEV, LON), bf16),
            pltpu.VMEM((WIDE // LANE, CELLS, LANE), f32),
            pltpu.VMEM((LEV, ROWS, WIDE), f32),
            pltpu.VMEM((LEV, ROWS, WIDE), f32),
            pltpu.VMEM((LEV, ROWS, WIDE), f32),
            pltpu.VMEM((LEV + 2, ROWS, WIDE), f32),
            pltpu.VMEM((LEV + 1, ROWS, WIDE), f32),
            pltpu.VMEM((LEV + 1, ROWS, WIDE), f32),
            pltpu.VMEM((LEV, ROWS, WIDE), f32),
            pltpu.VMEM((LEV, ROWS, WIDE), f32),
            pltpu.VMEM((4, LEV, WIDE), f32),
            pltpu.VMEM((2, LEV, WIDE), f32),
            pltpu.VMEM((LEV, WIDE), f32),
            pltpu.SemaphoreType.DMA((4,)),
            pltpu.SemaphoreType.DMA((NCHUNK,)),
            pltpu.SemaphoreType.DMA((4, NCHUNK)),
            pltpu.SemaphoreType.DMA((2,)),
            pltpu.SemaphoreType.DMA((2, 2)),
            pltpu.SemaphoreType.DMA((2,)),
            pltpu.SemaphoreType.DMA((2,)),
            pltpu.SemaphoreType.DMA((12,)),
        ],
        compiler_params=pltpu.CompilerParams(
            collective_id=shift, has_side_effects=True, vmem_limit_bytes=24 << 20
        ),
        name="transport",
    )(tracer, mass, flux, coup)


def per_device(tracer, air_mass, fluxes, diffusivity, input_slot):
    held = tracer.reshape(LEV, ROWS, LON)
    branches = [functools.partial(step, shift) for shift in range(SLOTS)]
    return lax.switch(input_slot[0], branches, held, air_mass, fluxes, diffusivity).reshape(tracer.shape)


def solution(mesh):
    placed = (
        P(None, "tracer", "band", None),
        P("tracer", None, "band", None),
        P("tracer", None, None, "band", None),
        P("tracer", None, "band", None),
        P(),
    )
    return jax.shard_map(
        per_device,
        mesh=mesh,
        in_specs=placed,
        out_specs=P(None, "tracer", "band", None),
        check_vma=False,
    )
```

time: 273 us -> 52.6 us (0.19)
  waiting for transfers between devices: 219 us -> 0 us
  Pallas kernels: 0 us -> 50.4 us
  starting transfers between devices: 22.7 us -> 0 us
  between operations: 14.3 us -> 0.05 us
  other arithmetic: 11.5 us -> 0 us
  local copies, waits for them, and re-layouts: 4.16 us -> 1.4 us
    psum x1 -> x0, waiting for transfers between devices: 200 us -> none  [from_root(): return lax.psum(block, axis)]
    pallas_call x0 -> x1, Pallas kernels: none -> 50.4 us  [step(): pl.pallas_call(functools.partial(step_kernel, shift), out_shape=jax.Shape...]
    ppermute x3 -> x0, starting transfers between devices: 22.7 us -> none  [the longest x1 7.85 us: from_behind(): return lax.ppermute(block, axis, route)]
    ppermute x3 -> x0, waiting for transfers between devices: 18.7 us -> none  [the longest x1 10.1 us: extended(): before = lax.ppermute(last, axis, up)]
    select_n x12 -> x0, other arithmetic: 5.73 us -> none  [the longest x2 2.76 us: from_root(): jnp.where(lax.axis_index(axis) == holder, block, jnp.zeros_like(block))]
  transfers between devices with their start and end apart: 4 -> 0, of which waited for: 4 -> 0; matrix products, arithmetic and copies ran while one was open for 0% -> 0% of each run, Pallas kernels for 0% -> 0%
where the time goes in v2:
time: 52.6 us; the launch traced here: 52.4 us
  Pallas kernels  50.4 us (96%)
  local copies, waits for them, and re-layouts  1.4 us (3%)
  loops' own time  0.58 us (1%)
    pallas_call x1, Pallas kernels, step(): pl.pallas_call(functools.partial(step_kernel, shift), out_shape=jax.Shape...  50.4 us
    unnamed x3, local copies, waits for them, and re-layouts  1.4 us

profile of v2, /device:TPU:7, one launch (start us, length us, event | category | flops | bytes accessed | tf_op | source)
XLA Modules:
  0.0 52.4 jit_solution(18287619319511857946)
XLA Ops:
  0.0 0.0 copy-start
  0.0 0.7 %copy-done = s32[32]{0:T(128)S(1)} copy-done((s32[32]{0:T(128)S(1)}, s32[32]{0:T(128)}, u32[]{:S(2)}) %copy-start) | copy-done | bytes 152
  0.7 51.0 %conditional.1 = (f32[16,1,8,720]{3,2,1,0:T(8,128)S(1)}) conditional(s32[]{:T(128)} %bitcast.48, (f32[16,8,720]{2,1,0:T(8,128)}, bf16[1,16,8,720]{3,2,1,0:T(8,128)(2,1)}, bf16[1,3,16,8,720]{4,3,2,1,0:T(8,128)(2,1)}, bf16[1,16,8,720]{3,2,1,0:T(8,128)(2,1)}) %tuple.118, (f32[16,8,720]{2,1,0:T(8,128)}, ...), branch_computations={%region_0.0_spmd, %region_1.0_spmd, %region_2.0_spmd, %region_3.0_... | conditional | bytes 8 | solution.py:540
  1.0 50.4 %transport.24 = f32[16,8,720]{2,1,0:T(8,128)S(1)} custom-call(f32[16,8,720]{2,1,0:T(8,128)} %get-tuple-element.183.x_hbm, bf16[1,16,8,720]{3,2,1,0:T(8,128)(2,1)} %get-tuple-element.184.mass_ref, bf16[1,3,16,8,720]{4,3,2,1,0:T(8,128)(2,1)} %get-tuple-element.185.flux_ref, bf16[1,16,8,720]{3,2,1,0:T(8,128)(2,1)} %get-tuple-element.186.coup_ref), custom_call_target="tpu_custom_call" | custom-call | tf_op jit(solution)/shard_map/cond/branch_8_fun/transport/pallas_call | solution.py:496
  51.7 0.7 %copy.56 = f32[16,1,8,720]{3,2,1,0:T(8,128)} copy(f32[16,1,8,720]{3,2,1,0:T(8,128)S(1)} %get-tuple-element.216) | data formatting | bytes 737280
Async XLA Ops:
  0.0 0.7 %copy-start = (s32[32]{0:T(128)S(1)}, s32[32]{0:T(128)}, u32[]{:S(2)}) copy-start(s32[32]{0:T(128)} %param.25) | copy-start | bytes 388

commit v3 on v2

--- a/solution.py
+++ b/solution.py
@@ -20,6 +20,7 @@
 CHUNK = 4
 PER_FIELD = LEV // CHUNK
 NCHUNK = 5 * PER_FIELD
+EARLY = 3 * PER_FIELD
 BELOW = 5
 ABOVE = 4
 
@@ -67,11 +68,16 @@
     def plane(i):
         return extended(edge[i].astype(f32))
 
-    for at, mass_at, east_at, out_of in ((0, 0, 2, lowest), (1, 1, 3, lowest), (2, 5, 7, highest), (3, 6, 8, highest)):
-        conc, _, inverse = advect_x(extended(halo[at].astype(f32)), plane(mass_at), plane(east_at))
+    def one_row(at, _):
+        upper = at // 2
+        mass_at = at + 3 * upper
+        conc, _, inverse = advect_x(extended(halo[at].astype(f32)), plane(mass_at), plane(mass_at + 2))
+        out_of = jnp.where(upper == 1, highest, lowest)
         side_c[at] = jnp.where(out_of, 0.0, conc)
-        if at in (1, 2):
-            side_i[at - 1] = jnp.where(out_of, 1.0, inverse)
+        side_i[at] = jnp.where(out_of, 1.0, inverse)
+        return 0
+
+    lax.fori_loop(0, 4, one_row, 0)
     side_f[...] = jnp.where(lowest, 0.0, plane(4))
 
 
@@ -108,7 +114,7 @@
     low_out = jnp.where(last, conc, spread(side_c, 0))
     high_out = jnp.where(first, conc, spread(side_c, 3))
     f_out = jnp.where(first, f_before, north)
-    i_out = jnp.where(first, spread(side_i, 0), spread(side_i, 1))
+    i_out = jnp.where(first, spread(side_i, 1), spread(side_i, 2))
     s_out = 0.25 * doubled_slope(c_out - low_out, high_out - c_out)
     from_out = c_out + (jnp.where(first, 1.0, -1.0) - f_out * i_out) * s_out
     moved = north * jnp.where(north > 0.0, ahead, jnp.where(last, from_out, higher(behind)))
@@ -141,33 +147,6 @@
     return slope_above, flux, moved, k_above, ratio_here, value_here, above, beyond, mass_above, inverse_above
 
 
-def in_pairs(body, carry=None):
-    def both(i, carry):
-        carry = body(2 * i, carry)
-        return body(2 * i + 1, carry)
-
-    return lax.fori_loop(0, LEV // 2, both, carry)
-
-
-def vertical_and_solve(met, out, conc2, mass2, inverse2, ratio, value):
-    zero = jnp.zeros((ROWS, WIDE), jnp.float32)
-    for beyond in range(2):
-        conc2[LEV + beyond] = zero
-    mass2[LEV] = zero
-    inverse2[LEV] = zero
-    first_slope = 0.25 * doubled_slope(conc2[0], conc2[1] - conc2[0])
-    start = (first_slope, zero, zero, zero, zero, zero, conc2[0], conc2[1], mass2[0], inverse2[0])
-    in_pairs(lambda lev, carry: vertical(lev, carry, met, conc2, mass2, inverse2, ratio, value), start)
-
-    def back(i, above):
-        lev = LEV - 1 - i
-        result = value[lev] + ratio[lev] * above
-        out[lev] = result[:, :LON]
-        return result
-
-    in_pairs(back, zero)
-
-
 def row_plane(stage, row):
     parts = [stage[j, pl.ds(row, LEV, stride=ROWS), :] for j in range(WIDE // LANE)]
     parts[-1] = parts[-1][:, :LON % LANE]
@@ -181,11 +160,18 @@
         stage[j, :, :width] = field[:, j * LANE:j * LANE + width]
 
 
+def stride_tree(z, entry):
+    pos, length = z - entry, CHIPS - 1 - entry
+    even = pos % 2 == 0
+    parent_pos = jnp.where(even, pos - 2, jnp.where(pos < length, pos + 1, pos - 1))
+    return entry + parent_pos, even & (pos < length), even, z + jnp.minimum(2, length - pos)
+
+
 def step_kernel(
     shift, x_hbm, mass_ref, flux_ref, coup_ref, out,
     x_ref, met, edge, halo, hsend, proxy, esend, stage,
     conc1, mass1, inverse1, conc2, mass2, inverse2, ratio, value, side_c, side_i, side_f,
-    local_sem, main_recv, main_send, halo_recv, halo_send, proxy_sem, edge_recv, edge_send,
+    local_sem, out_sem, main_recv, main_send, halo_recv, halo_send, proxy_sem, edge_recv, edge_send,
 ):
     b = lax.axis_index("band")
     t = lax.axis_index("tracer")
@@ -203,24 +189,35 @@
     has_below = b > 0
     has_above = b < BANDS - 1
 
-    side = jnp.where(z >= k, 1, -1)
-    pos = jnp.where(z >= k, z - k, k - z)
-    length = jnp.where(z >= k, CHIPS - 1 - k, k)
-    hub = passes & (pos % 2 == 0)
-    child_far = hub & (pos + 2 <= length)
-    child_back = hub
-    child_last = hub & (pos + 1 == length)
-    odd_parent = jnp.where(pos < length, pos + 1, pos - 1)
-    parent_pos = jnp.where(pos % 2 == 0, pos - 2, odd_parent)
-    up_step = jnp.minimum(CHIPS - 1 - k, 2)
-    down_step = jnp.minimum(k, 2)
-    root_up = is_root & (up_step > 0)
-    root_down = is_root & (down_step > 0)
-
-    edge_hub = speaker & ((z == 2) | (z == 5))
-    edge_leaf = speaker & (z != 2) & (z != 5)
-    hub_z = jnp.where(z < 4, 2, 5)
-    far_z = jnp.where(z == 2, 0, 7)
+    above = z > k
+    pos = jnp.where(above, z - k, k - z)
+    length = jnp.where(above, CHIPS - 1 - k, k)
+    middle = (length + 1) // 2
+    after = length - middle
+    at_middle = passes & jnp.logical_not(above) & (pos == middle)
+    at_far = passes & jnp.logical_not(above) & (pos == middle + 2)
+    beyond_parent = jnp.where((after == 1) | (pos == middle + 2), middle, middle + 2)
+    down_parent = k - jnp.where(pos == middle, 0, jnp.where(pos < middle, pos + 1, beyond_parent))
+    stride_parent, stride_on, stride_back, stride_to = stride_tree(z, k)
+    main_parent = jnp.where(above, stride_parent, down_parent)
+    down_on = (at_middle & (after >= 1)) | (at_far & (length >= middle + 3))
+    down_back = (at_middle & (middle >= 2)) | (passes & jnp.logical_not(above) & (pos < middle) & (pos >= 2)) | at_far
+    child_on = jnp.where(above, passes & stride_on, down_on)
+    child_back = jnp.where(above, passes & stride_back, down_back)
+    on_to = jnp.where(above, stride_to, z - jnp.where(at_middle & (after >= 2), 2, 1))
+    back_to = jnp.where(above, z - 1, z + 1)
+    leaf = passes & jnp.logical_not(child_on | child_back)
+    root_up = is_root & (k < CHIPS - 1)
+    root_down = is_root & (k > 0)
+    up_to = jnp.minimum(k + 2, CHIPS - 1)
+    down_to = k - (k + 1) // 2
+
+    entry = z // 4 * 4 + 1
+    at_entry = speaker & (z == entry)
+    edge_on = speaker & ((z == entry) | (z == entry + 1))
+    edge_back = at_entry
+    edge_parent = jnp.where(z == entry + 2, z - 1, entry)
+
     tells = speaker & at_root
 
     def one(flag):
@@ -243,12 +240,12 @@
 
     neighbour = jnp.where(relay, t, mate)
     greet(b, mate)
-    greet(b, (k + side * parent_pos) * 2 + c, passes)
+    greet(b, main_parent * 2 + c, passes)
     greet(b - 1, neighbour, has_below)
     greet(b + 1, neighbour, has_above)
-    greet(b, hub_z * 2 + c, edge_leaf)
-    greet(b - 1, speaker_at_root(b - 1), edge_hub & has_below)
-    greet(b + 1, speaker_at_root(b + 1), edge_hub & has_above)
+    greet(b, edge_parent * 2 + c, speaker & jnp.logical_not(at_entry))
+    greet(b - 1, speaker_at_root(b - 1), at_entry & has_below)
+    greet(b + 1, speaker_at_root(b + 1), at_entry & has_above)
 
     x_load = pltpu.make_async_copy(x_hbm, x_ref, local_sem.at[3])
     x_load.start()
@@ -264,21 +261,18 @@
         for load in loads:
             load.start()
 
-    x_load.wait()
-    fill_stage(stage, x_ref[...])
-    for plane, row in enumerate((ROWS - 2, ROWS - 1, 0, 1)):
-        hsend[plane] = row_plane(stage, row)
-
     neighbours = one(has_below) + one(has_above)
-    pl.semaphore_wait(
-        barrier,
-        1
-        + one(child_far) + one(child_back) + one(child_last)
-        + one(root_up) + one(root_down)
-        + 2 * one(speaker) * neighbours
-        + 3 * one(edge_hub)
-        + 2 * one(tells) * neighbours,
-    )
+
+    def joined():
+        pl.semaphore_wait(
+            barrier,
+            1
+            + one(child_on) + one(child_back)
+            + one(root_up) + one(root_down)
+            + 2 * one(speaker) * neighbours
+            + one(edge_on) + one(edge_back)
+            + 2 * one(tells) * neighbours,
+        )
 
     def remote(src, dst, send_sem, recv_sem, band, tracer):
         return pltpu.make_async_remote_copy(
@@ -286,26 +280,80 @@
             device_id={"band": band, "tracer": tracer}, device_id_type=MESH,
         )
 
-    def main_copy(i, which, tracer):
-        piece = met.at[i // PER_FIELD, pl.ds(i % PER_FIELD * CHUNK, CHUNK)]
-        return remote(piece, piece, main_send.at[which, i], main_recv.at[i], b, tracer)
+    def piece_of(i):
+        late = i >= EARLY
+        which = jnp.where(late, 3 + (i - EARLY) % 2, i // PER_FIELD)
+        group = jnp.where(late, (i - EARLY) // 2, i % PER_FIELD)
+        return which, pl.ds(group * CHUNK, CHUNK)
+
+    def main_copy(i, which, tracer, src=None):
+        piece = met.at[piece_of(i)]
+        return remote(piece if src is None else src, piece, main_send.at[which, i], main_recv.at[i], b, tracer)
 
     def start_if(flag, copy):
         pl.when(flag)(copy.start)
 
+    mate_first = b % 2 == 1
+
+    def send_line(i, src):
+        start_if(root_up, main_copy(i, 0, up_to * 2 + c, src))
+        start_if(root_down, main_copy(i, 1, down_to * 2 + c, src))
+
+    def send_mate(i, src):
+        main_copy(i, 2, mate, src).start()
+
+    def mass_piece(i):
+        return mass_ref.at[0, piece_of(i)[1]]
+
+    def flux_piece(i):
+        which, part = piece_of(i)
+        return flux_ref.at[0, which - 1, part]
+
+    def coupling_piece(i):
+        return coup_ref.at[0, piece_of(i)[1]]
+
+    def each(lower, upper, stride, body):
+        def go(i, _):
+            body(lower + i * stride)
+            return 0
+
+        count = upper - lower
+        lax.fori_loop(0, (count if isinstance(count, int) else CHUNK) // stride, go, 0)
+
+    @pl.when(is_root)
+    def _():
+        joined()
+
+        @pl.when(mate_first)
+        def _():
+            each(0, PER_FIELD, 1, lambda i: send_mate(i, mass_piece(i)))
+            each(PER_FIELD, EARLY, 1, lambda i: send_mate(i, flux_piece(i)))
+
+        def send(i, src):
+            send_line(i, src)
+
+            @pl.when(jnp.logical_not(mate_first))
+            def _():
+                send_mate(i, src)
+
+        each(0, PER_FIELD, 1, lambda i: send(i, mass_piece(i)))
+        each(PER_FIELD, EARLY, 1, lambda i: send(i, flux_piece(i)))
+
+        def last(i):
+            for at, src in ((i, flux_piece(i)), (i + 1, coupling_piece(i + 1))):
+                send_line(at, src)
+                send_mate(at, src)
+
+        each(EARLY, NCHUNK, 2, last)
+
+    x_load.wait()
+    fill_stage(stage, x_ref[...])
+    for plane, row in enumerate((ROWS - 2, ROWS - 1, 0, 1)):
+        hsend[plane] = row_plane(stage, row)
+
+    pl.when(jnp.logical_not(is_root))(joined)
+
     proxy_copy = remote(hsend, proxy, proxy_sem.at[0], proxy_sem.at[1], b, mate)
-
-    @pl.when(is_root)
-    def _():
-        def send(i, _):
-            start_if(root_up, main_copy(i, 0, (z + up_step) * 2 + c))
-            start_if(root_down, main_copy(i, 1, (z - down_step) * 2 + c))
-            main_copy(i, 3, mate).start()
-            return 0
-
-        for load, lower, upper in zip(loads, (0, 1, 4), (1, 4, 5), strict=True):
-            load.wait()
-            lax.fori_loop(lower * PER_FIELD, upper * PER_FIELD, send, 0)
 
     @pl.when(relay)
     def _():
@@ -313,40 +361,25 @@
 
     def handed(i):
         return (
-            (child_far, main_copy(i, 0, (z + 2 * side) * 2 + c)),
-            (child_back, main_copy(i, 1, (z - side) * 2 + c)),
-            (child_last, main_copy(i, 2, (z + side) * 2 + c)),
-            (None, main_copy(i, 3, mate)),
+            (child_on, main_copy(i, 0, on_to * 2 + c)),
+            (child_back, main_copy(i, 1, back_to * 2 + c)),
+            (None, main_copy(i, 2, mate)),
         )
 
-    def pass_on(i, _):
+    def arrive(i):
         main_copy(i, 0, mate).wait_recv()
+
+    def pass_on(i):
+        arrive(i)
         for flag, copy in handed(i):
             if flag is None:
                 copy.start()
             else:
                 start_if(flag, copy)
-        return 0
-
-    def levels(j, _):
-        for lev in (2 * j, 2 * j + 1):
-            longitude(lev, x_ref, met, conc1, mass1, inverse1)
-        return 0
 
     @pl.when(passes)
     def _():
-        lax.fori_loop(0, 2 * PER_FIELD, pass_on, 0)
-
-        def both(j, _):
-            pass_on(2 * PER_FIELD + j, 0)
-            return levels(j, 0)
-
-        lax.fori_loop(0, LEV // 2, both, 0)
-        lax.fori_loop(2 * PER_FIELD + LEV // 2, NCHUNK, pass_on, 0)
-
-    @pl.when(is_root)
-    def _():
-        lax.fori_loop(0, LEV // 2, levels, 0)
+        each(0, 2 * PER_FIELD, 1, pass_on)
 
     def halo_copy(lower, own, band, tracer):
         part = pl.ds(0 if lower else 2, 2)
@@ -361,29 +394,47 @@
         for lower, band, flag in ((True, b + 1, has_above), (False, b - 1, has_below))
     )
 
-    def edge_copy(which, lower, band, tracer, own):
-        part = pl.ds(0, BELOW) if lower else pl.ds(BELOW, ABOVE)
+    parts = ((0, 2, True), (5, 2, False), (2, 3, True), (7, 2, False))
+
+    def edge_copy(which, at, band, tracer, own):
+        first, count, _ = parts[at]
+        part = pl.ds(first, count)
         return remote(
-            (esend if own else edge).at[part], edge.at[part],
-            edge_send.at[which], edge_recv.at[0 if lower else 1], band, tracer,
+            (esend if own else edge).at[part], edge.at[part], edge_send.at[which, at], edge_recv.at[at], band, tracer
         )
 
-    edge_out = tuple(
-        (tells & flag, edge_copy(which + (0 if lower else 1), lower, band, chip * 2 + line_core, True))
-        for which, chip in ((0, 2), (2, 5))
-        for lower, band, flag in ((True, b + 1, has_above), (False, b - 1, has_below))
-    )
-
-    def edge_relay(lower):
-        first = 4 if lower else 8
+    def edge_out(at):
+        lower = parts[at][2]
+        band = b + 1 if lower else b - 1
+        flag = tells & (has_above if lower else has_below)
+        return tuple((flag, edge_copy(3 + half, at, band, (4 * half + 1) * 2 + line_core, True)) for half in (0, 1))
+
+    def edge_relay(at):
         return (
-            (edge_hub, edge_copy(first, lower, b, (z - 1) * 2 + c, False)),
-            (edge_hub, edge_copy(first + 1, lower, b, (z + 1) * 2 + c, False)),
-            (edge_hub, edge_copy(first + 2, lower, b, far_z * 2 + c, False)),
-            (None, edge_copy(first + 3, lower, b, mate, False)),
+            (edge_on, edge_copy(0, at, b, (z + 1) * 2 + c, False)),
+            (edge_back, edge_copy(1, at, b, (z - 1) * 2 + c, False)),
+            (None, edge_copy(2, at, b, mate, False)),
         )
 
+    def tell(at):
+        for flag, copy in edge_out(at):
+            start_if(flag, copy)
+
+    def has_part(at):
+        return has_below if parts[at][2] else has_above
+
     sides = ((True, has_below), (False, has_above))
+
+    def take_edges():
+        for at in range(4):
+            @pl.when(has_part(at))
+            def _(at=at):
+                edge_copy(0, at, b, mate, False).wait_recv()
+                for flag, copy in edge_relay(at):
+                    if flag is None:
+                        copy.start()
+                    else:
+                        start_if(flag, copy)
 
     @pl.when(speaker)
     def _():
@@ -401,37 +452,42 @@
                 (2, ((ROWS - 1, 4),)),
             )
             for field, places in plan:
-                for i in range(PER_FIELD):
-                    main_copy(field * PER_FIELD + i, 0, mate).wait_recv()
+                each(field * PER_FIELD, (field + 1) * PER_FIELD, 1, arrive)
                 fill_stage(stage, met[field].astype(jnp.float32))
                 for row, place in places:
                     esend[place] = row_plane(stage, row)
-            for flag, copy in edge_out:
-                start_if(flag, copy)
-
-        for lower, present in sides:
-            @pl.when(present)
-            def _(lower=lower):
-                edge_copy(0, lower, b, mate, False).wait_recv()
-                for flag, copy in edge_relay(lower):
-                    if flag is None:
-                        copy.start()
-                    else:
-                        start_if(flag, copy)
-
-        def arrived(i, _):
-            main_copy(i, 0, mate).wait_recv()
-            return 0
-
-        first = jnp.where(at_root, 3 * PER_FIELD, 0)
-        lax.fori_loop(first, jnp.maximum(first, 2 * PER_FIELD), arrived, 0)
-        lax.fori_loop(0, LEV // 2, levels, 0)
-        lax.fori_loop(jnp.maximum(first, 2 * PER_FIELD), NCHUNK, arrived, 0)
+                if field == 0:
+                    tell(0)
+                    tell(1)
+            tell(2)
+            tell(3)
+
+        pl.when(edge_on)(take_edges)
+        pl.when(jnp.logical_not(at_root))(lambda: each(0, 2 * PER_FIELD, 1, arrive))
+
+    @pl.when(is_root)
+    def _():
+        for load in loads:
+            load.wait()
+
+    def along(group):
+        pl.when(passes)(lambda: pass_on(2 * PER_FIELD + group))
+        pl.when(speaker & jnp.logical_not(at_root))(lambda: arrive(2 * PER_FIELD + group))
+
+        def pair(lower):
+            for lev in (lower, lower + 1):
+                longitude(lev, x_ref, met, conc1, mass1, inverse1)
+
+        each(group * CHUNK, (group + 1) * CHUNK, 2, pair)
+
+    each(0, PER_FIELD, 1, along)
+    pl.when(speaker & jnp.logical_not(edge_on))(take_edges)
+    pl.when(passes & jnp.logical_not(leaf))(lambda: each(EARLY, NCHUNK, 1, pass_on))
 
     @pl.when(relay)
     def _():
-        for lower, present in sides:
-            pl.when(present)(edge_copy(0, lower, b, mate, False).wait_recv)
+        for at in range(4):
+            pl.when(has_part(at))(edge_copy(0, at, b, mate, False).wait_recv)
 
     for lower, present in sides:
         pl.when(present)(halo_copy(lower, True, b, mate).wait_recv)
@@ -447,7 +503,49 @@
         return 0
 
     lax.fori_loop(0, LEV // 2, across, 0)
-    vertical_and_solve(met, out, conc2, mass2, inverse2, ratio, value)
+    zero = jnp.zeros((ROWS, WIDE), jnp.float32)
+    for beyond in range(2):
+        conc2[LEV + beyond] = zero
+    mass2[LEV] = zero
+    inverse2[LEV] = zero
+
+    def eliminate(group, carry):
+        @pl.when(leaf)
+        def _():
+            pass_on(EARLY + 2 * group)
+            pass_on(EARLY + 2 * group + 1)
+
+        @pl.when(speaker)
+        def _():
+            arrive(EARLY + 2 * group)
+            arrive(EARLY + 2 * group + 1)
+
+        def pair(i, carry):
+            for lev in (0, 1):
+                carry = vertical(group * CHUNK + 2 * i + lev, carry, met, conc2, mass2, inverse2, ratio, value)
+            return carry
+
+        return lax.fori_loop(0, CHUNK // 2, pair, carry)
+
+    first_slope = 0.25 * doubled_slope(conc2[0], conc2[1] - conc2[0])
+    start = (first_slope, zero, zero, zero, zero, zero, conc2[0], conc2[1], mass2[0], inverse2[0])
+    lax.fori_loop(0, PER_FIELD, eliminate, start)
+
+    def result(group):
+        part = pl.ds(group * CHUNK, CHUNK)
+        return pltpu.make_async_copy(x_ref.at[part], out.at[part], out_sem.at[group])
+
+    def back(i, above):
+        group = PER_FIELD - 1 - i
+        for lev in range(CHUNK - 1, -1, -1):
+            lev = group * CHUNK + lev
+            above = value[lev] + ratio[lev] * above
+            x_ref[lev] = above[:, :LON]
+        result(group).start()
+        return above
+
+    lax.fori_loop(0, PER_FIELD, back, zero)
+    each(0, PER_FIELD, 1, lambda i: result(i).wait())
 
     @pl.when(relay)
     def _():
@@ -455,12 +553,15 @@
 
     @pl.when(speaker)
     def _():
-        for flag, copy in halos + edge_out:
+        for flag, copy in halos:
             pl.when(flag)(copy.wait_send)
-        for lower, present in sides:
-            @pl.when(present)
-            def _(lower=lower):
-                for flag, copy in edge_relay(lower):
+        for at in range(4):
+            for flag, copy in edge_out(at):
+                pl.when(flag)(copy.wait_send)
+
+            @pl.when(has_part(at))
+            def _(at=at):
+                for flag, copy in edge_relay(at):
                     if flag is None:
                         copy.wait_send()
                     else:
@@ -468,36 +569,33 @@
 
     @pl.when(is_root)
     def _():
-        def done(i, _):
+        def done(i):
             pl.when(root_up)(main_copy(i, 0, mate).wait_send)
             pl.when(root_down)(main_copy(i, 1, mate).wait_send)
-            main_copy(i, 3, mate).wait_send()
-            return 0
-
-        lax.fori_loop(0, NCHUNK, done, 0)
+            main_copy(i, 2, mate).wait_send()
+
+        each(0, NCHUNK, 1, done)
 
     @pl.when(passes)
     def _():
-        def done(i, _):
+        def done(i):
             for flag, copy in handed(i):
                 if flag is None:
                     copy.wait_send()
                 else:
                     pl.when(flag)(copy.wait_send)
-            return 0
-
-        lax.fori_loop(0, NCHUNK, done, 0)
+
+        each(0, NCHUNK, 1, done)
 
 
 def step(shift, tracer, mass, flux, coup):
-    vmem = pl.BlockSpec(memory_space=pltpu.VMEM)
     hbm = pl.BlockSpec(memory_space=pl.ANY)
     bf16, f32 = jnp.bfloat16, jnp.float32
     return pl.pallas_call(
         functools.partial(step_kernel, shift),
         out_shape=jax.ShapeDtypeStruct((LEV, ROWS, LON), f32),
         in_specs=[hbm, hbm, hbm, hbm],
-        out_specs=vmem,
+        out_specs=hbm,
         scratch_shapes=[
             pltpu.VMEM((LEV, ROWS, LON), f32),
             pltpu.VMEM((5, LEV, ROWS, LON), bf16),
@@ -516,16 +614,17 @@
             pltpu.VMEM((LEV, ROWS, WIDE), f32),
             pltpu.VMEM((LEV, ROWS, WIDE), f32),
             pltpu.VMEM((4, LEV, WIDE), f32),
-            pltpu.VMEM((2, LEV, WIDE), f32),
+            pltpu.VMEM((4, LEV, WIDE), f32),
             pltpu.VMEM((LEV, WIDE), f32),
             pltpu.SemaphoreType.DMA((4,)),
+            pltpu.SemaphoreType.DMA((PER_FIELD,)),
             pltpu.SemaphoreType.DMA((NCHUNK,)),
-            pltpu.SemaphoreType.DMA((4, NCHUNK)),
+            pltpu.SemaphoreType.DMA((3, NCHUNK)),
             pltpu.SemaphoreType.DMA((2,)),
             pltpu.SemaphoreType.DMA((2, 2)),
             pltpu.SemaphoreType.DMA((2,)),
-            pltpu.SemaphoreType.DMA((2,)),
-            pltpu.SemaphoreType.DMA((12,)),
+            pltpu.SemaphoreType.DMA((4,)),
+            pltpu.SemaphoreType.DMA((5, 4)),
         ],
         compiler_params=pltpu.CompilerParams(
             collective_id=shift, has_side_effects=True, vmem_limit_bytes=24 << 20

time: 52.6 us -> 49 us (0.932)
  the two profiles are of different devices: /device:TPU:7 before, /device:TPU:17 now
where the time goes in v3:
time: 49 us; the launch traced here: 48.8 us
  Pallas kernels  47.1 us (96%)
  local copies, waits for them, and re-layouts  1.4 us (3%)
    pallas_call x1, Pallas kernels, step(): pl.pallas_call(functools.partial(step_kernel, shift), out_shape=jax.Shape...  47.1 us
    unnamed x3, local copies, waits for them, and re-layouts  1.4 us

profile of v3, /device:TPU:17, one launch (start us, length us, event | category | flops | bytes accessed | tf_op | source)
XLA Modules:
  0.0 48.8 jit_solution(5348354979427758472)
XLA Ops:
  0.0 0.0 copy-start
  0.0 0.7 %copy-done = s32[32]{0:T(128)S(1)} copy-done((s32[32]{0:T(128)S(1)}, s32[32]{0:T(128)}, u32[]{:S(2)}) %copy-start) | copy-done | bytes 152
  0.7 47.3 %conditional.1 = (f32[16,1,8,720]{3,2,1,0:T(8,128)S(1)}) conditional(s32[]{:T(128)} %bitcast.48, (f32[16,8,720]{2,1,0:T(8,128)}, bf16[1,16,8,720]{3,2,1,0:T(8,128)(2,1)}, bf16[1,3,16,8,720]{4,3,2,1,0:T(8,128)(2,1)}, bf16[1,16,8,720]{3,2,1,0:T(8,128)(2,1)}) %tuple.118, (f32[16,8,720]{2,1,0:T(8,128)}, ...), branch_computations={%region_0.0_spmd, %region_1.0_spmd, %region_2.0_spmd, %region_3.0_... | conditional | bytes 8 | solution.py:639
  0.9 47.1 %transport.30 = f32[16,8,720]{2,1,0:T(8,128)S(1)} custom-call(f32[16,8,720]{2,1,0:T(8,128)} %get-tuple-element.207.x_hbm, bf16[1,16,8,720]{3,2,1,0:T(8,128)(2,1)} %get-tuple-element.208.mass_ref, bf16[1,3,16,8,720]{4,3,2,1,0:T(8,128)(2,1)} %get-tuple-element.209.flux_ref, bf16[1,16,8,720]{3,2,1,0:T(8,128)(2,1)} %get-tuple-element.210.coup_ref), custom_call_target="tpu_custom_call" | custom-call | tf_op jit(solution)/shard_map/cond/branch_14_fun/transport/pallas_call | solution.py:594
  48.0 0.7 %copy.56 = f32[16,1,8,720]{3,2,1,0:T(8,128)} copy(f32[16,1,8,720]{3,2,1,0:T(8,128)S(1)} %get-tuple-element.216) | data formatting | bytes 737280
Async XLA Ops:
  0.0 0.7 %copy-start = (s32[32]{0:T(128)S(1)}, s32[32]{0:T(128)}, u32[]{:S(2)}) copy-start(s32[32]{0:T(128)} %param.25) | copy-start | bytes 388

commit v4 on v3

--- a/solution.py
+++ b/solution.py
@@ -296,8 +296,8 @@
     mate_first = b % 2 == 1
 
     def send_line(i, src):
+        start_if(root_down, main_copy(i, 1, down_to * 2 + c, src))
         start_if(root_up, main_copy(i, 0, up_to * 2 + c, src))
-        start_if(root_down, main_copy(i, 1, down_to * 2 + c, src))
 
     def send_mate(i, src):
         main_copy(i, 2, mate, src).start()

time: 49 us -> 48.8 us (level)
  the two profiles are of different devices: /device:TPU:17 before, /device:TPU:25 now
where the time goes in v4:
time: 48.8 us; the launch traced here: 48.2 us
  Pallas kernels  46.5 us (95%)
  local copies, waits for them, and re-layouts  1.4 us (3%)
    pallas_call x1, Pallas kernels, step(): pl.pallas_call(functools.partial(step_kernel, shift), out_shape=jax.Shape...  46.5 us
    unnamed x3, local copies, waits for them, and re-layouts  1.4 us

profile of v4, /device:TPU:25, one launch (start us, length us, event | category | flops | bytes accessed | tf_op | source)
XLA Modules:
  0.0 48.2 jit_solution(14364561516467513587)
XLA Ops:
  0.0 0.0 copy-start
  0.0 0.7 %copy-done = s32[32]{0:T(128)S(1)} copy-done((s32[32]{0:T(128)S(1)}, s32[32]{0:T(128)}, u32[]{:S(2)}) %copy-start) | copy-done | bytes 152
  0.7 46.8 %conditional.1 = (f32[16,1,8,720]{3,2,1,0:T(8,128)S(1)}) conditional(s32[]{:T(128)} %bitcast.48, (f32[16,8,720]{2,1,0:T(8,128)}, bf16[1,16,8,720]{3,2,1,0:T(8,128)(2,1)}, bf16[1,3,16,8,720]{4,3,2,1,0:T(8,128)(2,1)}, bf16[1,16,8,720]{3,2,1,0:T(8,128)(2,1)}) %tuple.118, (f32[16,8,720]{2,1,0:T(8,128)}, ...), branch_computations={%region_0.0_spmd, %region_1.0_spmd, %region_2.0_spmd, %region_3.0_... | conditional | bytes 8 | solution.py:639
  0.9 46.5 %transport.28 = f32[16,8,720]{2,1,0:T(8,128)S(1)} custom-call(f32[16,8,720]{2,1,0:T(8,128)} %get-tuple-element.199.x_hbm, bf16[1,16,8,720]{3,2,1,0:T(8,128)(2,1)} %get-tuple-element.200.mass_ref, bf16[1,3,16,8,720]{4,3,2,1,0:T(8,128)(2,1)} %get-tuple-element.201.flux_ref, bf16[1,16,8,720]{3,2,1,0:T(8,128)(2,1)} %get-tuple-element.202.coup_ref), custom_call_target="tpu_custom_call" | custom-call | tf_op jit(solution)/shard_map/cond/branch_12_fun/transport/pallas_call | solution.py:594
  47.5 0.7 %copy.56 = f32[16,1,8,720]{3,2,1,0:T(8,128)} copy(f32[16,1,8,720]{3,2,1,0:T(8,128)S(1)} %get-tuple-element.216) | data formatting | bytes 737280
Async XLA Ops:
  0.0 0.7 %copy-start = (s32[32]{0:T(128)S(1)}, s32[32]{0:T(128)}, u32[]{:S(2)}) copy-start(s32[32]{0:T(128)} %param.25) | copy-start | bytes 388
